TPU v7x, 256 devices: a whole 4x4x8 slice. The times are simulated.
256 devices in a mesh: seq: 64 (over z, y_hi, x), head: 4 (over y_lo, core).
Axes of the slice: x: 4, y: 4 (y_hi: 2, y_lo: 2; y = y_hi * 2 + y_lo), z: 8, core: 2. Of those that a mesh axis runs over, the one named last changes fastest.
Arguments:
- queries: bfloat16 [32768, 4096], P('seq', 'head'), may hold values from -100 to 100
- keys: bfloat16 [32768, 1024], P('seq', 'head'), may hold values from -5 to 5
- values: bfloat16 [32768, 1024], P('seq', 'head'), may hold values from -6 to 6
- lengths: int32 [16], replicated, may hold values from 1 to 4096, 32768 in all
- out_weight: bfloat16 [4096, 4096], P('head'), may hold values from -0.125 to 0.125
Outputs:
- mixed: bfloat16 [32768, 4096], P('seq', 'head')
Inputs may be any that keep to these rules, and one draw needn't show every extreme that they name: `lengths`: each document holds at least one token and the longest holds exactly 4096.
All inputs are finite; a program needn't handle non-finite values.
Results may differ from a plain program's by a relative error of at most 0.019.
Values may be sent and summed in bfloat16 or wider, within the bound.
A program may use at most 64 MiB of HBM per device.

v0:
```python
import math

import jax
import jax.numpy as jnp
from jax import lax
from jax.sharding import PartitionSpec as P

HEAD_WIDTH = 128
HORIZON = 8


def from_behind(x, axis, by):
    length = lax.axis_size(axis)
    pairs = [(i, i + by) for i in range(length) if 0 <= i + by < length]
    return lax.ppermute(x, axis, pairs)


def on_device(queries, keys, values, lengths, out_weight):
    rows = queries.shape[0]
    heads = keys.shape[1] // HEAD_WIDTH
    group = queries.shape[1] // keys.shape[1]
    first = lax.axis_index("seq") * rows
    ends = jnp.cumsum(lengths)
    factor = 1.0 / math.sqrt(HEAD_WIDTH)

    def docs_of(places):
        return jnp.sum((ends[None, :] <= places[:, None]).astype(jnp.int32), axis=1)

    def attend(state, info, k_piece, v_piece, start):
        q_mat, q_pos, q_doc, q_first = info
        count = k_piece.shape[0]
        width = math.gcd(count, 512)
        k_all = k_piece.reshape(count, heads, HEAD_WIDTH)
        v_all = v_piece.reshape(count, heads, HEAD_WIDTH)

        def inner(index, inner_state):
            top, total, accum = inner_state
            offset = index * width
            k_pos = start + offset + jnp.arange(width, dtype=jnp.int32)
            k_doc = docs_of(k_pos)
            allowed = (q_doc[:, None] == k_doc[None, :]) & (k_pos[None, :] <= q_pos[:, None])
            scores = (
                jnp.einsum("qgrd,kgd->grqk", q_mat, k_all, preferred_element_type=jnp.float32)
                * factor
            )
            scores = jnp.where(allowed, scores, -1e30)
            new_top = jnp.maximum(top, jnp.max(scores, axis=-1))
            expo = jnp.where(allowed, jnp.exp(scores - new_top[..., None]), 0.0)
            shrink = jnp.exp(top - new_top)
            total = total * shrink + jnp.sum(expo, axis=-1)
            update = jnp.einsum(
                "zmcp,pzf->czmf",
                expo.astype(jnp.bfloat16),
                v_all,
                preferred_element_type=jnp.float32,
            )
            accum = accum * jnp.transpose(shrink, (2, 0, 1))[..., None] + update
            return (new_top, total, accum)

        return lax.fori_loop(0, count // width, inner, state)

    def fold_for(state, info, pieces, start):
        k_piece, v_piece = pieces
        q_doc = info[2]
        q_first = info[3]
        count = k_piece.shape[0]
        last_doc = docs_of(jnp.reshape(start + count - 1, (1,)))[0]
        needed = (start >= 0) & (start <= q_first + rows - 1) & (last_doc >= q_doc[0])
        return lax.cond(
            needed,
            lambda inner_state: attend(inner_state, info, k_piece, v_piece, start),
            lambda inner_state: inner_state,
            state,
        )

    q_pos = first + jnp.arange(rows, dtype=jnp.int32)
    home = (queries.reshape(rows, heads, group, HEAD_WIDTH), q_pos, docs_of(q_pos), first)
    start_state = (
        jnp.full((heads, group, rows), -1e30, jnp.float32),
        jnp.zeros((heads, group, rows), jnp.float32),
        jnp.zeros((rows, heads, group, HEAD_WIDTH), jnp.float32),
    )
    state = fold_for(start_state, home, (keys, values), first)
    reach = min(HORIZON, lax.axis_size("seq") // 2)
    stacked = jnp.stack((keys, values))

    def travel(index, packed):
        inner_state, moving = packed
        moving = from_behind(moving, "seq", 1)
        start = first - (index + 1) * rows
        return (fold_for(inner_state, home, (moving[0], moving[1]), start), moving)

    state, unused = lax.fori_loop(0, reach, travel, (state, stacked))
    top, total, accum = state
    attended = (
        (accum / jnp.transpose(total, (2, 0, 1))[..., None])
        .astype(jnp.bfloat16)
        .reshape(rows, heads * group * HEAD_WIDTH)
    )
    partial_terms = jnp.dot(attended, out_weight, preferred_element_type=jnp.float32)
    return lax.psum_scatter(
        partial_terms.astype(jnp.bfloat16), "head", scatter_dimension=1, tiled=True
    )


def solution(mesh):
    in_specs = (P("seq", "head"), P("seq", "head"), P("seq", "head"), P(), P("head", None))
    out_specs = P("seq", "head")
    return jax.shard_map(
        on_device, mesh=mesh, in_specs=in_specs, out_specs=out_specs, check_vma=False
    )
```

profile of v0, /device:TPU:1, one launch (start us, length us, event | category | flops | bytes accessed | tf_op | source)
XLA Modules:
  0.0 324.3 jit_solution(16938080825247952171)
XLA Ops:
  6.5 0.7 copy.30
  7.3 0.6 fusion.31
  8.0 0.6 slice.35
  8.6 1.5 copy.31
  10.1 0.7 copy.35
  10.8 1.1 copy.33
  11.9 1.1 copy.34
  14.4 18.4 %conditional.2 = (f32[2,4,512]{2,1,0:T(4,128)}, f32[2,4,512]{2,1,0:T(4,128)S(1)}, f32[512,2,4,128]{3,0,2,1:T(8,128)}) conditional(s32[]{:T(128)} %convert_element_type.73, () %tuple.57, (s32[512]{0:T(512)S(1)}, s32[16]{0:T(128)S(1)}, s32[]{:T(128)}, s32[512]{0:T(512)S(1)}, bf16[512,256]{1,0:T(8,128)(2,1)}, ...), branch_computations={%region_3.4_spmd, %region_4.8_spmd} | conditional | flops 1102356480 | bytes 65730708 | solution.py:69
  14.8 1.0 reshape.83
  15.8 4.8 %fusion.2 = (f32[2,4,512]{2,1,0:T(4,128)S(1)}, f32[2,512,512,4]{2,1,3,0:T(8,128)}) fusion(pred[512,512]{0,1:T(8,128)(4,1)S(1)} %compare_and_fusion, bf16[512,2,4,128]{0,3,2,1:T(8,128)(2,1)S(1)} %get-tuple-element.609, bf16[512,2,128,1]{2,1,0,3:T(2,128)(2,1)S(1)} %bitcast.74), kind=kOutput, calls=%fused_computation.3 | convolution fusion | flops 543158272 | bytes 9977856 | tf_op jit(solution)/shard_map/cond/branch_1_fun/while/body/eval_jaxpr/qgrd,kgd->grqk/dot_general | solution.py:43
  20.6 0.6 fusion.13
  21.3 7.8 %bitcast_add_fusion = f32[512,2,4,128]{3,0,2,1:T(8,128)} fusion(f32[2,512,512,4]{2,1,3,0:T(8,128)} %get-tuple-element.657, f32[2,4,512]{2,1,0:T(4,128)} %get-tuple-element.734, pred[512,512]{0,1:T(8,128)(4,1)S(1)} %compare_and_fusion, f32[512,2,4]{0,2,1:T(4,128)S(1)} %get-tuple-element.646, bf16[512,2,128,1]{2,1,0,3:T(2,128)(2,1)S(1)} %bitcast.80), kind=kOutput, calls=%fused_computation.8 | convolution fusion | flops 547880960 | bytes 11042816 | tf_op jit(solution)/shard_map/cond/branch_1_fun/while/body/eval_jaxpr/zmcp,pzf->czmf/dot_general | solution.py:51
  29.1 2.7 fusion.4
  31.9 0.7 fusion.14
  32.8 144.0 %while.32 = (s32[]{:T(128)}, f32[2,4,512]{2,1,0:T(4,128)}, f32[2,4,512]{2,1,0:T(4,128)S(1)}, f32[512,2,4,128]{3,0,2,1:T(8,128)}, bf16[2,512,256]{1,2,0:T(8,128)(...) while((s32[]{:T(128)}, f32[2,4,512]{2,1,0:T(4,128)}, ...), condition=%wide.region_15.0_spmd.clone.clone, body=%wide.region_8.15_spmd.clone.clone.sunk | while | flops 1102877184 | bytes 36459032 | solution.py:93
  32.8 4.0 %collective-permute-start = (bf16[2,512,256]{1,2,0:T(8,128)(2,1)S(1)}, bf16[2,512,256]{1,2,0:T(8,128)(2,1)S(1)}, u32[]{:S(2)}, u32[]{:S(2)}) collective-permute-start(bf16[2,512,256]{1,2,0:T(8,128)(2,1)S(1)} %get-tuple-element.755), channel_id=1, source_target_pairs={{0,4},{4,8},{8,12},{12,16},{16,20},{20,24},{24,28},{28,32},{32,36}... | collective-permute-start | bytes 1572872 | tf_op jit(solution)/shard_map/while/body/eval_jaxpr/ppermute | solution.py:15
  36.8 0.5 slice.41
  37.4 0.6 fusion.40
  39.2 8.2 %collective-permute-done = bf16[2,512,256]{1,2,0:T(8,128)(2,1)S(1)} collective-permute-done((bf16[2,512,256]{1,2,0:T(8,128)(2,1)S(1)}, bf16[2,512,256]{1,2,0:T(8,128)(2,1)S(1)}, u32[]{:S(2)}, u32[]{:S(2)}) %collective-permute-start) | collective-permute-done | bytes 524320 | tf_op jit(solution)/shard_map/while/body/eval_jaxpr/ppermute | solution.py:15
  47.4 16.1 %collective-permute-start = (bf16[2,512,256]{1,2,0:T(8,128)(2,1)S(1)}, bf16[2,512,256]{1,2,0:T(8,128)(2,1)S(1)}, u32[]{:S(2)}, u32[]{:S(2)}) collective-permute-start(bf16[2,512,256]{1,2,0:T(8,128)(2,1)S(1)} %get-tuple-element.755), channel_id=1, source_target_pairs={{0,4},{4,8},{8,12},{12,16},{16,20},{20,24},{24,28},{28,32},{32,36}... | collective-permute-start | bytes 1572872 | tf_op jit(solution)/shard_map/while/body/eval_jaxpr/ppermute | solution.py:15
  63.6 0.5 slice.41
  64.1 0.6 fusion.40
  65.9 7.2 %collective-permute-done = bf16[2,512,256]{1,2,0:T(8,128)(2,1)S(1)} collective-permute-done((bf16[2,512,256]{1,2,0:T(8,128)(2,1)S(1)}, bf16[2,512,256]{1,2,0:T(8,128)(2,1)S(1)}, u32[]{:S(2)}, u32[]{:S(2)}) %collective-permute-start) | collective-permute-done | bytes 524320 | tf_op jit(solution)/shard_map/while/body/eval_jaxpr/ppermute | solution.py:15
  73.2 4.1 %collective-permute-start = (bf16[2,512,256]{1,2,0:T(8,128)(2,1)S(1)}, bf16[2,512,256]{1,2,0:T(8,128)(2,1)S(1)}, u32[]{:S(2)}, u32[]{:S(2)}) collective-permute-start(bf16[2,512,256]{1,2,0:T(8,128)(2,1)S(1)} %get-tuple-element.755), channel_id=1, source_target_pairs={{0,4},{4,8},{8,12},{12,16},{16,20},{20,24},{24,28},{28,32},{32,36}... | collective-permute-start | bytes 1572872 | tf_op jit(solution)/shard_map/while/body/eval_jaxpr/ppermute | solution.py:15
  77.4 0.5 slice.41
  77.9 0.6 fusion.40
  79.7 6.3 %collective-permute-done = bf16[2,512,256]{1,2,0:T(8,128)(2,1)S(1)} collective-permute-done((bf16[2,512,256]{1,2,0:T(8,128)(2,1)S(1)}, bf16[2,512,256]{1,2,0:T(8,128)(2,1)S(1)}, u32[]{:S(2)}, u32[]{:S(2)}) %collective-permute-start) | collective-permute-done | bytes 524320 | tf_op jit(solution)/shard_map/while/body/eval_jaxpr/ppermute | solution.py:15
  86.1 4.1 %collective-permute-start = (bf16[2,512,256]{1,2,0:T(8,128)(2,1)S(1)}, bf16[2,512,256]{1,2,0:T(8,128)(2,1)S(1)}, u32[]{:S(2)}, u32[]{:S(2)}) collective-permute-start(bf16[2,512,256]{1,2,0:T(8,128)(2,1)S(1)} %get-tuple-element.755), channel_id=1, source_target_pairs={{0,4},{4,8},{8,12},{12,16},{16,20},{20,24},{24,28},{28,32},{32,36}... | collective-permute-start | bytes 1572872 | tf_op jit(solution)/shard_map/while/body/eval_jaxpr/ppermute | solution.py:15
  90.3 0.5 slice.41
  90.8 0.6 fusion.40
  92.6 5.4 %collective-permute-done = bf16[2,512,256]{1,2,0:T(8,128)(2,1)S(1)} collective-permute-done((bf16[2,512,256]{1,2,0:T(8,128)(2,1)S(1)}, bf16[2,512,256]{1,2,0:T(8,128)(2,1)S(1)}, u32[]{:S(2)}, u32[]{:S(2)}) %collective-permute-start) | collective-permute-done | bytes 524320 | tf_op jit(solution)/shard_map/while/body/eval_jaxpr/ppermute | solution.py:15
  98.1 18.1 %collective-permute-start = (bf16[2,512,256]{1,2,0:T(8,128)(2,1)S(1)}, bf16[2,512,256]{1,2,0:T(8,128)(2,1)S(1)}, u32[]{:S(2)}, u32[]{:S(2)}) collective-permute-start(bf16[2,512,256]{1,2,0:T(8,128)(2,1)S(1)} %get-tuple-element.755), channel_id=1, source_target_pairs={{0,4},{4,8},{8,12},{12,16},{16,20},{20,24},{24,28},{28,32},{32,36}... | collective-permute-start | bytes 1572872 | tf_op jit(solution)/shard_map/while/body/eval_jaxpr/ppermute | solution.py:15
  116.3 0.5 slice.41
  116.8 0.6 fusion.40
  118.6 4.5 %collective-permute-done = bf16[2,512,256]{1,2,0:T(8,128)(2,1)S(1)} collective-permute-done((bf16[2,512,256]{1,2,0:T(8,128)(2,1)S(1)}, bf16[2,512,256]{1,2,0:T(8,128)(2,1)S(1)}, u32[]{:S(2)}, u32[]{:S(2)}) %collective-permute-start) | collective-permute-done | bytes 524320 | tf_op jit(solution)/shard_map/while/body/eval_jaxpr/ppermute | solution.py:15
  123.2 7.7 %collective-permute-start = (bf16[2,512,256]{1,2,0:T(8,128)(2,1)S(1)}, bf16[2,512,256]{1,2,0:T(8,128)(2,1)S(1)}, u32[]{:S(2)}, u32[]{:S(2)}) collective-permute-start(bf16[2,512,256]{1,2,0:T(8,128)(2,1)S(1)} %get-tuple-element.755), channel_id=1, source_target_pairs={{0,4},{4,8},{8,12},{12,16},{16,20},{20,24},{24,28},{28,32},{32,36}... | collective-permute-start | bytes 1572872 | tf_op jit(solution)/shard_map/while/body/eval_jaxpr/ppermute | solution.py:15
  130.9 0.5 slice.41
  131.5 0.6 fusion.40
  133.3 3.7 %collective-permute-done = bf16[2,512,256]{1,2,0:T(8,128)(2,1)S(1)} collective-permute-done((bf16[2,512,256]{1,2,0:T(8,128)(2,1)S(1)}, bf16[2,512,256]{1,2,0:T(8,128)(2,1)S(1)}, u32[]{:S(2)}, u32[]{:S(2)}) %collective-permute-start) | collective-permute-done | bytes 524320 | tf_op jit(solution)/shard_map/while/body/eval_jaxpr/ppermute | solution.py:15
  137.0 19.8 %collective-permute-start = (bf16[2,512,256]{1,2,0:T(8,128)(2,1)S(1)}, bf16[2,512,256]{1,2,0:T(8,128)(2,1)S(1)}, u32[]{:S(2)}, u32[]{:S(2)}) collective-permute-start(bf16[2,512,256]{1,2,0:T(8,128)(2,1)S(1)} %get-tuple-element.755), channel_id=1, source_target_pairs={{0,4},{4,8},{8,12},{12,16},{16,20},{20,24},{24,28},{28,32},{32,36}... | collective-permute-start | bytes 1572872 | tf_op jit(solution)/shard_map/while/body/eval_jaxpr/ppermute | solution.py:15
  157.3 0.6 fusion.40
  159.2 3.7 %collective-permute-done = bf16[2,512,256]{1,2,0:T(8,128)(2,1)S(1)} collective-permute-done((bf16[2,512,256]{1,2,0:T(8,128)(2,1)S(1)}, bf16[2,512,256]{1,2,0:T(8,128)(2,1)S(1)}, u32[]{:S(2)}, u32[]{:S(2)}) %collective-permute-start) | collective-permute-done | bytes 524320 | tf_op jit(solution)/shard_map/while/body/eval_jaxpr/ppermute | solution.py:15
  162.9 7.8 %collective-permute-start = (bf16[2,512,256]{1,2,0:T(8,128)(2,1)S(1)}, bf16[2,512,256]{1,2,0:T(8,128)(2,1)S(1)}, u32[]{:S(2)}, u32[]{:S(2)}) collective-permute-start(bf16[2,512,256]{1,2,0:T(8,128)(2,1)S(1)} %get-tuple-element.755), channel_id=1, source_target_pairs={{0,4},{4,8},{8,12},{12,16},{16,20},{20,24},{24,28},{28,32},{32,36}... | collective-permute-start | bytes 1572872 | tf_op jit(solution)/shard_map/while/body/eval_jaxpr/ppermute | solution.py:15
  171.2 0.6 fusion.40
  173.1 3.7 %collective-permute-done = bf16[2,512,256]{1,2,0:T(8,128)(2,1)S(1)} collective-permute-done((bf16[2,512,256]{1,2,0:T(8,128)(2,1)S(1)}, bf16[2,512,256]{1,2,0:T(8,128)(2,1)S(1)}, u32[]{:S(2)}, u32[]{:S(2)}) %collective-permute-start) | collective-permute-done | bytes 524320 | tf_op jit(solution)/shard_map/while/body/eval_jaxpr/ppermute | solution.py:15
  176.8 1.9 copy.36
  179.0 9.5 %convolution_convert_fusion = bf16[512,4096]{1,0:T(8,128)(2,1)} fusion(bf16[512,1024]{0,1:T(8,128)(2,1)S(1)} %bitcast.73, bf16[1024,4096]{1,0:T(8,128)(2,1)} %param.15), kind=kOutput, calls=%fused_computation.42 | convolution fusion | flops 4297064448 | bytes 13631488 | tf_op jit(solution)/shard_map/dot_general | solution.py:100
  188.5 128.9 %reduce-scatter.2.cloned.1.call-done = bf16[512,1024]{1,0:T(8,128)(2,1)} async-done(((bf16[512,4096]{1,0:T(8,128)(2,1)}), bf16[512,1024]{1,0:T(8,128)(2,1)}) %reduce-scatter.2.cloned.1.call-update) | async-done | bytes 1048592 | tf_op jit(solution)/shard_map/reduce_scatter | solution.py:101
  (41 shorter events, 2.3 us)
Async XLA Ops:
  6.5 310.9 %reduce-scatter.2.cloned.1.call-start = ((), (), s32[]{:S(2)}) async-start(), calls=%async_computation.1 | async-start | bytes 5242880 | tf_op jit(solution)/shard_map/reduce_scatter | solution.py:101
  14.4 6.8 %copy-start.1 = (bf16[512,256]{1,0:T(8,128)(2,1)S(1)}, bf16[512,256]{1,0:T(8,128)(2,1)}, u32[]{:S(2)}) copy-start(bf16[512,256]{1,0:T(8,128)(2,1)} %get-tuple-element.497) | copy-start | bytes 786436 | tf_op jit(solution)/shard_map/cond
  21.3 7.8 %copy-start = (f32[2,512,512,4]{2,1,3,0:T(8,128)S(1)}, f32[2,512,512,4]{2,1,3,0:T(8,128)}, u32[]{:S(2)}) copy-start(f32[2,512,512,4]{2,1,3,0:T(8,128)} %get-tuple-element.657) | copy-start | bytes 25165828 | tf_op jit(solution)/shard_map/cond
  32.8 14.5 %collective-permute-start = (bf16[2,512,256]{1,2,0:T(8,128)(2,1)S(1)}, bf16[2,512,256]{1,2,0:T(8,128)(2,1)S(1)}, u32[]{:S(2)}, u32[]{:S(2)}) collective-permute-start(bf16[2,512,256]{1,2,0:T(8,128)(2,1)S(1)} %get-tuple-element.755), channel_id=1, source_target_pairs={{0,4},{4,8},{8,12},{12,16},{16,20},{20,24},{24,28},{28,32},{32,36}... | collective-permute-start | bytes 1572872 | tf_op jit(solution)/shard_map/while/body/eval_jaxpr/ppermute | solution.py:15
  47.4 25.8 %collective-permute-start = (bf16[2,512,256]{1,2,0:T(8,128)(2,1)S(1)}, bf16[2,512,256]{1,2,0:T(8,128)(2,1)S(1)}, u32[]{:S(2)}, u32[]{:S(2)}) collective-permute-start(bf16[2,512,256]{1,2,0:T(8,128)(2,1)S(1)} %get-tuple-element.755), channel_id=1, source_target_pairs={{0,4},{4,8},{8,12},{12,16},{16,20},{20,24},{24,28},{28,32},{32,36}... | collective-permute-start | bytes 1572872 | tf_op jit(solution)/shard_map/while/body/eval_jaxpr/ppermute | solution.py:15
  73.2 12.8 %collective-permute-start = (bf16[2,512,256]{1,2,0:T(8,128)(2,1)S(1)}, bf16[2,512,256]{1,2,0:T(8,128)(2,1)S(1)}, u32[]{:S(2)}, u32[]{:S(2)}) collective-permute-start(bf16[2,512,256]{1,2,0:T(8,128)(2,1)S(1)} %get-tuple-element.755), channel_id=1, source_target_pairs={{0,4},{4,8},{8,12},{12,16},{16,20},{20,24},{24,28},{28,32},{32,36}... | collective-permute-start | bytes 1572872 | tf_op jit(solution)/shard_map/while/body/eval_jaxpr/ppermute | solution.py:15
  86.1 11.9 %collective-permute-start = (bf16[2,512,256]{1,2,0:T(8,128)(2,1)S(1)}, bf16[2,512,256]{1,2,0:T(8,128)(2,1)S(1)}, u32[]{:S(2)}, u32[]{:S(2)}) collective-permute-start(bf16[2,512,256]{1,2,0:T(8,128)(2,1)S(1)} %get-tuple-element.755), channel_id=1, source_target_pairs={{0,4},{4,8},{8,12},{12,16},{16,20},{20,24},{24,28},{28,32},{32,36}... | collective-permute-start | bytes 1572872 | tf_op jit(solution)/shard_map/while/body/eval_jaxpr/ppermute | solution.py:15
  98.1 25.0 %collective-permute-start = (bf16[2,512,256]{1,2,0:T(8,128)(2,1)S(1)}, bf16[2,512,256]{1,2,0:T(8,128)(2,1)S(1)}, u32[]{:S(2)}, u32[]{:S(2)}) collective-permute-start(bf16[2,512,256]{1,2,0:T(8,128)(2,1)S(1)} %get-tuple-element.755), channel_id=1, source_target_pairs={{0,4},{4,8},{8,12},{12,16},{16,20},{20,24},{24,28},{28,32},{32,36}... | collective-permute-start | bytes 1572872 | tf_op jit(solution)/shard_map/while/body/eval_jaxpr/ppermute | solution.py:15
  123.2 13.8 %collective-permute-start = (bf16[2,512,256]{1,2,0:T(8,128)(2,1)S(1)}, bf16[2,512,256]{1,2,0:T(8,128)(2,1)S(1)}, u32[]{:S(2)}, u32[]{:S(2)}) collective-permute-start(bf16[2,512,256]{1,2,0:T(8,128)(2,1)S(1)} %get-tuple-element.755), channel_id=1, source_target_pairs={{0,4},{4,8},{8,12},{12,16},{16,20},{20,24},{24,28},{28,32},{32,36}... | collective-permute-start | bytes 1572872 | tf_op jit(solution)/shard_map/while/body/eval_jaxpr/ppermute | solution.py:15
  137.0 25.8 %collective-permute-start = (bf16[2,512,256]{1,2,0:T(8,128)(2,1)S(1)}, bf16[2,512,256]{1,2,0:T(8,128)(2,1)S(1)}, u32[]{:S(2)}, u32[]{:S(2)}) collective-permute-start(bf16[2,512,256]{1,2,0:T(8,128)(2,1)S(1)} %get-tuple-element.755), channel_id=1, source_target_pairs={{0,4},{4,8},{8,12},{12,16},{16,20},{20,24},{24,28},{28,32},{32,36}... | collective-permute-start | bytes 1572872 | tf_op jit(solution)/shard_map/while/body/eval_jaxpr/ppermute | solution.py:15
  162.9 13.8 %collective-permute-start = (bf16[2,512,256]{1,2,0:T(8,128)(2,1)S(1)}, bf16[2,512,256]{1,2,0:T(8,128)(2,1)S(1)}, u32[]{:S(2)}, u32[]{:S(2)}) collective-permute-start(bf16[2,512,256]{1,2,0:T(8,128)(2,1)S(1)} %get-tuple-element.755), channel_id=1, source_target_pairs={{0,4},{4,8},{8,12},{12,16},{16,20},{20,24},{24,28},{28,32},{32,36}... | collective-permute-start | bytes 1572872 | tf_op jit(solution)/shard_map/while/body/eval_jaxpr/ppermute | solution.py:15
Sparse Core Ops, SparseCore 0:
  188.7 128.6 reduce-scatter.1
where the time goes:
time: 326 us; the launch traced here: 324 us
  waiting for transfers between devices  172 us (53%)
  starting transfers between devices  81.8 us (25%)
  matrix products  22.1 us (7%)
  between operations  14.8 us (5%)
  local copies, waits for them, and re-layouts  13.3 us (4%)
  other arithmetic  10.5 us (3%)
  loops' own time  10.3 us (3%)
    reduce_scatter x1, waiting for transfers between devices, on_device(): lax.psum_scatter(partial_terms.astype(jnp.bfloat16), 'head', scatter_dime...  129 us
    ppermute x8, starting transfers between devices, from_behind(): return lax.ppermute(x, axis, pairs)  81.8 us
    ppermute x8, waiting for transfers between devices, from_behind(): return lax.ppermute(x, axis, pairs)  42.6 us
    another operation x1, loops' own time, on_device(): state, unused = lax.fori_loop(0, reach, travel, (state, stacked))  10 us
    dot_general x1, matrix products, on_device(): jnp.dot(attended, out_weight, preferred_element_type=jnp.float32)  9.48 us
    dot_general x1, matrix products, inner(): jnp.einsum('zmcp,pzf->czmf', expo.astype(jnp.bfloat16), v_all, preferred_...  7.84 us
  transfers between devices with their start and end apart: 9, of which 9 were waited for; matrix products, arithmetic and copies ran while one was open for 3% of the time, Pallas kernels for 0%

commit v1 on v0

v1 whole, which is shorter than its diff:
```python
import functools
import math

import jax
import jax.numpy as jnp
from jax import lax
from jax.experimental import pallas as pl
from jax.experimental.pallas import tpu as pltpu
from jax.sharding import PartitionSpec as P

HEAD = 128
GROUP = 4
ROWS = 512
BLOCK = 4 * ROWS
WINDOW = 3 * BLOCK
TILE = 512
DOCS = 16
STEPS = 8
SCALE = math.log2(math.e) / math.sqrt(HEAD)
LOW = -1e30
MESH = pl.DeviceIdType.MESH
NT = (((1,), (1,)), ((), ()))
ORDER = (0, 1, 3, 2)


def kernel(
    len_ref, q_hbm, k_hbm, v_hbm, w_hbm, out_ref,
    v_loc, vt, w, kv, q, thr, scores, acc, att_out, att, near_out, near_in,
    cross_out, cross_in, part, own,
    load_sem, kv_send, kv_recv, q_send, q_recv, z_send, z_recv, y_send, y_recv,
    sib_send, sib_recv, att_send, att_recv, near_send, near_recv, cross_send, cross_recv,
):
    s = lax.axis_index("seq")
    h = lax.axis_index("head")
    x = lax.rem(s, 4)
    yh = lax.rem(s // 4, 2)
    z = s // 8
    depth = lax.axis_size("seq") // 8
    yl = h // 2
    c = lax.rem(h, 2)

    def at(x_, c_):
        return (z * 8 + yh * 4 + x_, yl * 2 + c_)

    sibling = at(x, 1 - c)
    above = (lax.rem(z + 1, depth) * 8 + yh * 4 + x, h)
    below = (lax.rem(z + depth - 1, depth) * 8 + yh * 4 + x, h)
    across = (z * 8 + (1 - yh) * 4 + x, h)
    facing = (s, (1 - yl) * 2 + c)

    v_copy = pltpu.make_async_copy(v_hbm, v_loc, load_sem.at[0])
    w_copy = pltpu.make_async_copy(w_hbm, w, load_sem.at[1])
    v_copy.start()
    w_copy.start()

    barrier = pltpu.get_barrier_semaphore()
    partners = [sibling, above, below, across, facing]
    for d in (1, 2, 3):
        for e in (0, 1):
            partners.append(at(lax.rem(x + d, 4), e))
    for partner in partners:
        pl.semaphore_signal(barrier, inc=1, device_id=partner, device_id_type=MESH)

    n_at = lax.broadcasted_iota(jnp.int32, (STEPS, HEAD), 0)
    r_at = lax.broadcasted_iota(jnp.int32, (STEPS, HEAD), 1)
    begin = (s // 4) * BLOCK
    place = begin + (3 - (n_at & 3)) * ROWS + (n_at >> 2) * 256 + c * HEAD + r_at
    end = jnp.int32(0)
    start = jnp.zeros((STEPS, HEAD), jnp.int32)
    for d in range(DOCS):
        end = end + len_ref[d]
        start = jnp.where(place >= end, end, start)
    thr[...] = start - (begin - 2 * BLOCK)

    v_copy.wait()
    for i in range(2):
        for b in range(4):
            piece = v_loc[b * 128:(b + 1) * 128, i * 128:(i + 1) * 128]
            vt[i, b * 128:(b + 1) * 128, :] = piece.astype(jnp.float32).T.astype(jnp.bfloat16)

    pl.semaphore_wait(barrier, len(partners))

    def remote(src, dst, send, recv, device):
        return pltpu.make_async_remote_copy(
            src_ref=src, dst_ref=dst, send_sem=send, recv_sem=recv,
            device_id=device, device_id_type=MESH,
        )

    def each_way(is_self, copy, src, dst, recv):
        @pl.when(is_self)
        def _():
            pltpu.make_async_copy(src, dst, recv).start()

        @pl.when(jnp.logical_not(is_self))
        def _():
            copy.start()

    def arrived(dst, recv):
        pltpu.make_async_copy(dst, dst, recv).wait()

    def kv_at(kind, slot, shard):
        return kv.at[kind, pl.ds(pl.multiple_of(slot * BLOCK + shard * ROWS, ROWS), ROWS)]

    exchanged = []
    for kind in range(2):
        for i in range(2):
            src = k_hbm.at[:, pl.ds(i * HEAD, HEAD)] if kind == 0 else vt.at[i]
            dst = kv_at(kind, 2, x)
            is_self = (2 * c + i == x) & (c == kind)
            copy = remote(src, dst, kv_send.at[kind, i], kv_recv.at[x], at(2 * c + i, kind))
            each_way(is_self, copy, src, dst, kv_recv.at[x])
            exchanged.append((is_self, copy))
    for half in range(2):
        for i in range(2):
            for e in range(2):
                src = q_hbm.at[pl.ds(half * 256 + e * HEAD, HEAD), pl.ds(i * 512, 512)]
                step = half * 4 + 3 - x
                dst = q.at[step]
                is_self = (2 * c + i == x) & (c == e)
                copy = remote(src, dst, q_send.at[half, i, e], q_recv.at[step], at(2 * c + i, e))
                each_way(is_self, copy, src, dst, q_recv.at[step])
                exchanged.append((is_self, copy))

    def to_sibling(slot, shard):
        ref = kv_at(c, slot, shard)
        return remote(ref, ref, sib_send.at[slot, shard], sib_recv.at[slot, shard], sibling)

    def to_above(shard):
        return remote(kv_at(c, 2, shard), kv_at(c, 0, shard), z_send.at[shard], z_recv.at[shard], above)

    def to_across(slot, shard):
        return remote(kv_at(c, slot, shard), kv_at(c, 1, shard), y_send.at[shard], y_recv.at[shard], across)

    shards = [lax.rem(x + o, 4) for o in ORDER]
    for shard in shards:
        arrived(kv_at(c, 2, shard), kv_recv.at[shard])
        to_above(shard).start()

        @pl.when(yh == 0)
        def _():
            to_across(2, shard).start()

        to_sibling(2, shard).start()
    for shard in shards:
        arrived(kv_at(c, 0, shard), z_recv.at[shard])

        @pl.when(yh == 1)
        def _():
            to_across(0, shard).start()

        to_sibling(0, shard).start()
    for shard in shards:
        arrived(kv_at(c, 1, shard), y_recv.at[shard])
        to_sibling(1, shard).start()
    for slot in (2, 0, 1):
        for shard in shards:
            arrived(kv_at(1 - c, slot, shard), sib_recv.at[slot, shard])

    ones = jnp.ones((16, TILE), jnp.bfloat16)

    def attend(n):
        half = n // 4
        t = 3 - lax.rem(n, 4)
        low = pl.multiple_of(t * ROWS + half * 256 + c * HEAD, HEAD)
        arrived(q.at[n], q_recv.at[n])
        from_ = thr[pl.ds(n, 1), :]

        def weigh(off, count):
            q_all = jnp.concatenate([q[n, :, g * HEAD:(g + 1) * HEAD] for g in range(GROUP)], axis=0)
            return lax.dot_general(
                kv[0, pl.ds(off, count), :], q_all, NT, preferred_element_type=jnp.float32
            )

        def mix(off, count, p):
            blocks = [kv[1, pl.ds(pl.multiple_of(off + b * 128, 128), 128), :] for b in range(count // 128)]
            v_all = blocks[0] if len(blocks) == 1 else jnp.concatenate(blocks, axis=1)
            v_all = jnp.concatenate([v_all, ones[:, :count]], axis=0)
            return jnp.dot(v_all, p, preferred_element_type=jnp.float32)

        def masked(raw, allowed):
            bias = jnp.where(allowed, 0.0, LOW)
            return jnp.concatenate(
                [raw[:, g * HEAD:(g + 1) * HEAD] + bias for g in range(GROUP)], axis=1
            )

        diag = pl.multiple_of(low + 2 * BLOCK, HEAD)
        key_at = lax.broadcasted_iota(jnp.int32, (HEAD, HEAD), 0)
        row_at = lax.broadcasted_iota(jnp.int32, (HEAD, HEAD), 1)
        first = masked(weigh(diag, HEAD), (key_at <= row_at) & (key_at >= from_ - diag))
        top = jnp.max(first, axis=0, keepdims=True)
        acc[...] = mix(diag, HEAD, jnp.exp2((first - top) * SCALE).astype(jnp.bfloat16))

        def fill(slot, tile):
            off = pl.multiple_of(jnp.minimum(low + tile * TILE, WINDOW - TILE), HEAD)
            at_ = lax.broadcasted_iota(jnp.int32, (TILE, HEAD), 0)
            scores[slot] = masked(weigh(off, TILE), at_ >= from_ - off)

        fill(0, 0)

        def body(j, top):
            for u in range(4):
                tile = 4 * j + u
                fill((u + 1) % 2, tile + 1)
                now = scores[u % 2]
                new_top = jnp.maximum(top, jnp.max(now, axis=0, keepdims=True))
                p = jnp.exp2((now - new_top) * SCALE).astype(jnp.bfloat16)
                shrink = jnp.exp2((top - new_top) * SCALE)
                top = new_top
                off = pl.multiple_of(low + tile * TILE, HEAD)
                acc[...] = acc[...] * shrink + mix(off, TILE, p)
            return top

        lax.fori_loop(0, 2, body, top)
        done = acc[:HEAD] / acc[HEAD:HEAD + 1]
        for g in range(GROUP):
            att_out[n, :, g * HEAD:(g + 1) * HEAD] = done[:, g * HEAD:(g + 1) * HEAD].T.astype(jnp.bfloat16)

    def give_back(n):
        half = n // 4
        t = 3 - lax.rem(n, 4)
        dst = att.at[
            half,
            pl.ds(pl.multiple_of(c * HEAD, HEAD), HEAD),
            pl.ds(pl.multiple_of(lax.rem(x, 2) * 512, 512), 512),
        ]
        recv = att_recv.at[half, lax.rem(x, 2), c]
        copy = remote(att_out.at[n], dst, att_send.at[n], recv, at(t, x // 2))
        return (t == x) & (x // 2 == c), copy, att_out.at[n], dst, recv

    def near(half, which):
        return remote(
            near_out.at[half, which], near_in.at[half, which],
            near_send.at[half, which], near_recv.at[half, which], sibling,
        )

    def cross(half):
        return remote(
            cross_out.at[half], cross_in.at[half], cross_send.at[half], cross_recv.at[half], facing
        )

    def quarter(half, k, into):
        def body(j, carry):
            col = pl.multiple_of(k * 1024 + j * 512, 512)
            into(j * 512, jnp.dot(att[half], w[:, pl.ds(col, 512)], preferred_element_type=jnp.float32))
            return carry

        lax.fori_loop(0, 2, body, 0)

    def project(half):
        for e in range(2):
            for d in range(2):
                arrived(
                    att.at[half, pl.ds(d * HEAD, HEAD), pl.ds(e * 512, 512)], att_recv.at[half, e, d]
                )

        def to_near(which):
            def into(col, value):
                near_out[half, which, :, pl.ds(pl.multiple_of(col, 512), 512)] = value.astype(jnp.bfloat16)
            return into

        def to_part(col, value):
            part[:, pl.ds(pl.multiple_of(col, 512), 512)] = value

        def to_own(col, value):
            own[half, :, pl.ds(pl.multiple_of(col, 512), 512)] = value

        quarter(half, (1 - yl) * 2 + 1 - c, to_near(0))
        near(half, 0).start()
        quarter(half, (1 - yl) * 2 + c, to_part)
        near(half, 0).wait_recv()
        cross_out[half] = (part[...] + near_in[half, 0].astype(jnp.float32)).astype(jnp.bfloat16)
        cross(half).start()
        quarter(half, yl * 2 + 1 - c, to_near(1))
        near(half, 1).start()
        quarter(half, yl * 2 + c, to_own)

    w_copy.wait()

    def turn(n, carry):
        @pl.when(n < STEPS)
        def _():
            attend(n)
            is_self, copy, src, dst, recv = give_back(n)
            each_way(is_self, copy, src, dst, recv)

        late = n - (4 - x)

        @pl.when((late == 0) | (late == 4))
        def _():
            project(late // 4)

        return carry

    lax.fori_loop(0, STEPS + 1, turn, 0)

    for half in range(2):
        near(half, 1).wait_recv()
        cross(half).wait_recv()
        out_ref[half * 256:(half + 1) * 256, :] = (
            own[half] + near_in[half, 1].astype(jnp.float32) + cross_in[half].astype(jnp.float32)
        ).astype(jnp.bfloat16)

    for is_self, copy in exchanged:
        @pl.when(jnp.logical_not(is_self))
        def _():
            copy.wait_send()

    for shard in range(4):
        to_above(shard).wait_send()
        to_across(0, shard).wait_send()
        for slot in range(3):
            to_sibling(slot, shard).wait_send()
    for n in range(STEPS):
        is_self, copy, _, _, _ = give_back(n)

        @pl.when(jnp.logical_not(is_self))
        def _():
            copy.wait_send()

    for half in range(2):
        near(half, 0).wait_send()
        near(half, 1).wait_send()
        cross(half).wait_send()


def on_device(queries, keys, values, lengths, out_weight):
    bf16, f32 = jnp.bfloat16, jnp.float32
    dma = pltpu.SemaphoreType.DMA
    anywhere = pl.BlockSpec(memory_space=pl.ANY)
    return pl.pallas_call(
        kernel,
        out_shape=jax.ShapeDtypeStruct((ROWS, 1024), bf16),
        in_specs=[pl.BlockSpec(memory_space=pltpu.SMEM)] + [anywhere] * 4,
        out_specs=pl.BlockSpec(memory_space=pltpu.VMEM),
        scratch_shapes=[
            pltpu.VMEM((ROWS, 256), bf16),
            pltpu.VMEM((2, ROWS, HEAD), bf16),
            pltpu.VMEM((1024, 4096), bf16),
            pltpu.VMEM((2, WINDOW, HEAD), bf16),
            pltpu.VMEM((STEPS, HEAD, 512), bf16),
            pltpu.VMEM((STEPS, HEAD), jnp.int32),
            pltpu.VMEM((2, TILE, 512), f32),
            pltpu.VMEM((HEAD + 16, 512), f32),
            pltpu.VMEM((STEPS, HEAD, 512), bf16),
            pltpu.VMEM((2, 256, 1024), bf16),
            pltpu.VMEM((2, 2, 256, 1024), bf16),
            pltpu.VMEM((2, 2, 256, 1024), bf16),
            pltpu.VMEM((2, 256, 1024), bf16),
            pltpu.VMEM((2, 256, 1024), bf16),
            pltpu.VMEM((256, 1024), f32),
            pltpu.VMEM((2, 256, 1024), f32),
            dma((2,)),
            dma((2, 2)), dma((4,)),
            dma((2, 2, 2)), dma((STEPS,)),
            dma((4,)), dma((4,)),
            dma((4,)), dma((4,)),
            dma((3, 4)), dma((3, 4)),
            dma((STEPS,)), dma((2, 2, 2)),
            dma((2, 2)), dma((2, 2)),
            dma((2,)), dma((2,)),
        ],
        compiler_params=pltpu.CompilerParams(
            collective_id=0, has_side_effects=True, vmem_limit_bytes=56 * 2**20
        ),
        name="attend_and_project",
    )(lengths, queries, keys, values, out_weight)


def solution(mesh):
    in_specs = (P("seq", "head"), P("seq", "head"), P("seq", "head"), P(), P("head", None))
    return jax.shard_map(
        on_device, mesh=mesh, in_specs=in_specs, out_specs=P("seq", "head"), check_vma=False
    )
```

time: 326 us -> 105 us (0.32)
  waiting for transfers between devices: 172 us -> 0 us
  Pallas kernels: 0 us -> 103 us
  starting transfers between devices: 81.8 us -> 0 us
  matrix products: 22.1 us -> 0 us
  between operations: 14.8 us -> 0.01 us
  local copies, waits for them, and re-layouts: 13.3 us -> 2.26 us
  other arithmetic: 10.5 us -> 0 us
  loops' own time: 10.3 us -> 0 us
    reduce_scatter x1 -> x0, waiting for transfers between devices: 129 us -> none  [on_device(): lax.psum_scatter(partial_terms.astype(jnp.bfloat16), 'head', scatter_dime...]
    pallas_call x0 -> x1, Pallas kernels: none -> 103 us  [on_device(): pl.pallas_call(kernel, out_shape=jax.ShapeDtypeStruct((ROWS, 1024), bf16)...]
    ppermute x8 -> x0, starting transfers between devices: 81.8 us -> none  [from_behind(): return lax.ppermute(x, axis, pairs)]
    ppermute x8 -> x0, waiting for transfers between devices: 42.6 us -> none  [from_behind(): return lax.ppermute(x, axis, pairs)]
    dot_general x3 -> x0, matrix products: 22.1 us -> none  [the longest x1 9.48 us: on_device(): jnp.dot(attended, out_weight, preferred_element_type=jnp.float32)]
    another operation x10 -> x0, loops' own time: 10.3 us -> none  [the longest x1 10 us: on_device(): state, unused = lax.fori_loop(0, reach, travel, (state, stacked))]
    reduce_sum x11 -> x0, other arithmetic: 7.89 us -> none  [the longest x10 5.17 us: docs_of(): return jnp.sum((ends[None, :] <= places[:, None]).astype(jnp.int32), axis=1)]
    slice x9 -> x0, local copies, waits for them, and re-layouts: 4.9 us -> none  [fold_for(): q_doc[0]]
  transfers between devices with their start and end apart: 9 -> 0, of which waited for: 9 -> 0; matrix products, arithmetic and copies ran while one was open for 3% -> 0% of each run, Pallas kernels for 0% -> 0%
where the time goes in v1:
time: 105 us
  Pallas kernels  103 us (98%)
  local copies, waits for them, and re-layouts  2.26 us (2%)
    pallas_call x1, Pallas kernels, on_device(): pl.pallas_call(kernel, out_shape=jax.ShapeDtypeStruct((ROWS, 1024), bf16)...  103 us
    unnamed x1, local copies, waits for them, and re-layouts  2.26 us

profile of v1, /device:TPU:1, one launch (start us, length us, event | category | flops | bytes accessed | tf_op | source)
XLA Modules:
  0.0 104.9 jit_solution(14674015921837640700)
XLA Ops:
  0.0 102.6 %attend_and_project.1 = bf16[512,1024]{1,0:T(8,128)(2,1)} custom-call(s32[16]{0:T(128)} %len_ref.1, bf16[512,1024]{1,0:T(8,128)(2,1)} %q_hbm.1, bf16[512,256]{1,0:T(8,128)(2,1)} %k_hbm.1, bf16[512,256]{1,0:T(8,128)(2,1)} %v_hbm.1, bf16[1024,4096]{1,0:T(8,128)(2,1)} %w_hbm.1), custom_call_target="tpu_custom_call" | custom-call | tf_op jit(solution)/shard_map/attend_and_project/pallas_call | solution.py:330
  102.6 2.3 %copy.7 = bf16[512,1024]{1,0:T(8,128)(2,1)} copy(bf16[512,1024]{1,0:T(8,128)(2,1)} %attend_and_project.1) | data formatting | bytes 2097152

commit v2 on v1

v2 whole, which is shorter than its diff:
```python
import functools
import math

import jax
import jax.numpy as jnp
from jax import lax
from jax.experimental import pallas as pl
from jax.experimental.pallas import tpu as pltpu
from jax.sharding import PartitionSpec as P

HEAD = 128
GROUP = 4
ROWS = 512
BLOCK = 4 * ROWS
WINDOW = 3 * BLOCK
TILE = 512
DOCS = 16
STEPS = 8
PART = 128
SCALE = math.log2(math.e) / math.sqrt(HEAD)
LOW = -1e30
MESH = pl.DeviceIdType.MESH
NT = (((1,), (1,)), ((), ()))
ORDER = (0, 1, 3, 2)


def kernel(
    len_ref, q_hbm, k_hbm, v_hbm, w_hbm, out_hbm,
    out_loc, v_loc, vt, w, kv, q, thr, scores, acc, tops, att_out, att, near_out, near_in,
    cross_out, cross_in, part, own,
    load_sem, kv_send, kv_recv, q_send, q_recv, z_send, z_recv, y_send, y_recv,
    sib_send, sib_recv, att_send, att_recv, near_send, near_recv, cross_send, cross_recv, out_sem,
):
    s = lax.axis_index("seq")
    h = lax.axis_index("head")
    x = lax.rem(s, 4)
    yh = lax.rem(s // 4, 2)
    z = s // 8
    depth = lax.axis_size("seq") // 8
    yl = h // 2
    c = lax.rem(h, 2)

    def at(x_, c_):
        return (z * 8 + yh * 4 + x_, yl * 2 + c_)

    sibling = at(x, 1 - c)
    above = (lax.rem(z + 1, depth) * 8 + yh * 4 + x, h)
    below = (lax.rem(z + depth - 1, depth) * 8 + yh * 4 + x, h)
    across = (z * 8 + (1 - yh) * 4 + x, h)
    facing = (s, (1 - yl) * 2 + c)

    v_copy = pltpu.make_async_copy(v_hbm, v_loc, load_sem.at[0])
    w_copy = pltpu.make_async_copy(w_hbm, w, load_sem.at[1])
    v_copy.start()
    w_copy.start()

    barrier = pltpu.get_barrier_semaphore()
    partners = [sibling, above, below, across, facing]
    for d in (1, 2, 3):
        for e in (0, 1):
            partners.append(at(lax.rem(x + d, 4), e))
    for partner in partners:
        pl.semaphore_signal(barrier, inc=1, device_id=partner, device_id_type=MESH)

    n_at = lax.broadcasted_iota(jnp.int32, (STEPS, HEAD), 0)
    r_at = lax.broadcasted_iota(jnp.int32, (STEPS, HEAD), 1)
    begin = (s // 4) * BLOCK
    place = begin + ((n_at & 1) * 2 + (r_at >> 6)) * ROWS + (n_at >> 1) * PART + c * 64 + (r_at & 63)
    end = jnp.int32(0)
    start = jnp.zeros((STEPS, HEAD), jnp.int32)
    for d in range(DOCS):
        end = end + len_ref[d]
        start = jnp.where(place >= end, end, start)
    thr[...] = start - (begin - 2 * BLOCK)

    v_copy.wait()
    for i in range(2):
        for b in range(4):
            piece = v_loc[b * 128:(b + 1) * 128, i * 128:(i + 1) * 128]
            vt[i, b * 128:(b + 1) * 128, :] = piece.astype(jnp.float32).T.astype(jnp.bfloat16)

    pl.semaphore_wait(barrier, len(partners))

    def remote(src, dst, send, recv, device):
        return pltpu.make_async_remote_copy(
            src_ref=src, dst_ref=dst, send_sem=send, recv_sem=recv,
            device_id=device, device_id_type=MESH,
        )

    def each_way(is_self, copy, src, dst, recv):
        @pl.when(is_self)
        def _():
            pltpu.make_async_copy(src, dst, recv).start()

        @pl.when(jnp.logical_not(is_self))
        def _():
            copy.start()

    def arrived(dst, recv):
        pltpu.make_async_copy(dst, dst, recv).wait()

    def kv_at(kind, slot, shard):
        return kv.at[kind, pl.ds(pl.multiple_of(slot * BLOCK + shard * ROWS, ROWS), ROWS)]

    exchanged = []
    distant = []
    for kind in range(2):
        for i in range(2):
            src = k_hbm.at[:, pl.ds(i * HEAD, HEAD)] if kind == 0 else vt.at[i]
            dst = kv_at(kind, 2, x)
            is_self = (c + 2 * i == x) & (c == kind)
            is_far = lax.rem(c + 2 * i + 6 - x, 4) == 0
            copy = remote(src, dst, kv_send.at[kind, i], kv_recv.at[x], at(c + 2 * i, kind))

            each_way(is_self, copy, src, dst, kv_recv.at[x])

            exchanged.append((is_self, copy))
            distant.append((is_far, copy))

    def send_queries(part_):
        for e in range(2):
            for i in range(2):
                src = q_hbm.at[pl.ds(part_ * PART + e * 64, 64), pl.ds(i * 512, 512)]
                which = part_ * 2 + x // 2
                dst = q.at[which, pl.ds(pl.multiple_of(lax.rem(x, 2) * 64, 64), 64)]
                recv = q_recv.at[which, lax.rem(x, 2)]
                is_self = (c + 2 * i == x) & (c == e)
                copy = remote(src, dst, q_send.at[part_, i, e], recv, at(c + 2 * i, e))
                each_way(is_self, copy, src, dst, recv)
                exchanged.append((is_self, copy))

    def to_sibling(slot, shard):
        ref = kv_at(c, slot, shard)
        return remote(ref, ref, sib_send.at[slot, shard], sib_recv.at[slot, shard], sibling)

    def to_above(shard):
        return remote(kv_at(c, 2, shard), kv_at(c, 0, shard), z_send.at[shard], z_recv.at[shard], above)

    def to_across(slot, shard):
        return remote(kv_at(c, slot, shard), kv_at(c, 1, shard), y_send.at[shard], y_recv.at[shard], across)

    shards = [lax.rem(x + o, 4) for o in ORDER]
    def pass_own(shard):
        arrived(kv_at(c, 2, shard), kv_recv.at[shard])
        to_above(shard).start()

        @pl.when(yh == 0)
        def _():
            to_across(2, shard).start()

        to_sibling(2, shard).start()

    for shard in shards:
        pass_own(shard)
    send_queries(0)
    for part_ in range(1, 4):
        send_queries(part_)

    def pass_below(shard):
        arrived(kv_at(c, 0, shard), z_recv.at[shard])

        @pl.when(yh == 1)
        def _():
            to_across(0, shard).start()

        to_sibling(0, shard).start()

    def pass_across(shard):
        arrived(kv_at(c, 1, shard), y_recv.at[shard])
        to_sibling(1, shard).start()

    def from_sibling(slot):
        for shard in shards:
            arrived(kv_at(1 - c, slot, shard), sib_recv.at[slot, shard])

    pass_below(shards[0])
    pass_below(shards[1])
    from_sibling(2)

    ones = jnp.ones((16, TILE), jnp.bfloat16)

    def step_of(n):
        return (n // 2) * 2 + lax.rem(x // 2 + 1 + lax.rem(n, 2), 2)

    def low_of(which):
        return pl.multiple_of(lax.rem(which, 2) * 2 * ROWS + (which // 2) * PART, PART)

    def weigh(which, off, count):
        q_all = jnp.concatenate([q[which, :, g * HEAD:(g + 1) * HEAD] for g in range(GROUP)], axis=0)
        return lax.dot_general(
            kv[0, pl.ds(off, count), :], q_all, NT, preferred_element_type=jnp.float32
        )

    def mix(off, count, p):
        blocks = [kv[1, pl.ds(pl.multiple_of(off + b * 128, 128), 128), :] for b in range(count // 128)]
        v_all = blocks[0] if len(blocks) == 1 else jnp.concatenate(blocks, axis=1)
        v_all = jnp.concatenate([v_all, ones[:, :count]], axis=0)
        return jnp.dot(v_all, p, preferred_element_type=jnp.float32)

    def masked(raw, allowed):
        bias = jnp.where(allowed, 0.0, LOW)
        return jnp.concatenate(
            [raw[:, g * HEAD:(g + 1) * HEAD] + bias for g in range(GROUP)], axis=1
        )

    def allowed_at(which, off, count, causal):
        key_at = lax.broadcasted_iota(jnp.int32, (count, HEAD), 0)
        allowed = key_at >= thr[pl.ds(which, 1), :] - off
        if causal:
            col = lax.broadcasted_iota(jnp.int32, (1, HEAD), 1)
            place = low_of(which) + 2 * BLOCK + c * 64 + (col >> 6) * ROWS + (col & 63)
            allowed = allowed & (key_at <= place - off)
        return allowed

    def fill(slot, which, tile, causal=False):
        off = pl.multiple_of(low_of(which) + tile * TILE, HEAD)
        scores[slot] = masked(weigh(which, off, TILE), allowed_at(which, off, TILE, causal))

    def fold(slot, which, tile, top):
        now = scores[slot]
        new_top = jnp.maximum(top, jnp.max(now, axis=0, keepdims=True))
        p = jnp.exp2((now - new_top) * SCALE).astype(jnp.bfloat16)
        shrink = jnp.exp2((top - new_top) * SCALE)
        off = pl.multiple_of(low_of(which) + tile * TILE, HEAD)
        acc[which] = acc[which] * shrink + mix(off, TILE, p)
        return new_top

    def begin_step(which, tiles, extra=()):
        for e in range(2):
            arrived(q.at[which, pl.ds(e * 64, 64)], q_recv.at[which, e])
        diag = pl.multiple_of(low_of(which) + 9 * TILE, HEAD)
        first = masked(weigh(which, diag, HEAD), allowed_at(which, diag, HEAD, True))
        jobs = [(which, tile) for tile in tiles] + list(extra)
        fill(0, which, tiles[0], True)
        top = jnp.max(first, axis=0, keepdims=True)
        acc[which] = mix(diag, HEAD, jnp.exp2((first - top) * SCALE).astype(jnp.bfloat16))
        for u, (one, tile) in enumerate(jobs):
            if u + 1 < len(jobs):
                fill((u + 1) % 2, *jobs[u + 1])
            if u == len(tiles):
                tops[which] = top
                top = tops[one]
            top = fold(u % 2, one, tile, top)
        tops[jobs[-1][0]] = top

    def end_step(n):
        which = step_of(n)
        then = step_of(jnp.minimum(n + 1, STEPS - 1))
        base = 3 - 2 * lax.rem(which, 2)
        top = tops[which]
        for u in range(5):
            if u < 4:
                fill(u % 2, which, base + u + 1)
            else:
                fill(2, then, 3 - 2 * lax.rem(then, 2))
            top = fold((u - 1) % 2 if u else 2, which, base + u, top)
        done = acc[which, :HEAD] / acc[which, HEAD:HEAD + 1]
        for g in range(GROUP):
            att_out[n, :, g * HEAD:(g + 1) * HEAD] = done[:, g * HEAD:(g + 1) * HEAD].T.astype(jnp.bfloat16)

    def give_back(n, e):
        which = step_of(n)
        t = 2 * lax.rem(which, 2) + e
        src = att_out.at[n, pl.ds(e * 64, 64)]
        dst = att.at[
            which // 2,
            pl.ds(pl.multiple_of(c * 64, 64), 64),
            pl.ds(pl.multiple_of((x // 2) * 512, 512), 512),
        ]
        recv = att_recv.at[which // 2, x // 2, c]
        copy = remote(src, dst, att_send.at[n, e], recv, at(t, lax.rem(x, 2)))
        return (t == x) & (lax.rem(x, 2) == c), copy, src, dst, recv

    def near(half, which):
        return remote(
            near_out.at[half, which], near_in.at[half, which],
            near_send.at[half, which], near_recv.at[half, which], sibling,
        )

    def cross(half):
        return remote(
            cross_out.at[half], cross_in.at[half], cross_send.at[half], cross_recv.at[half], facing
        )

    def quarter(half, k, into):
        col = pl.multiple_of(k * 1024, 1024)
        into(jnp.dot(att[half], w[:, pl.ds(col, 1024)], preferred_element_type=jnp.float32))

    def project(half):
        for e in range(2):
            for d in range(2):
                arrived(
                    att.at[half, pl.ds(d * 64, 64), pl.ds(e * 512, 512)], att_recv.at[half, e, d]
                )

        def to_near(which):
            def into(value):
                near_out[half, which] = value.astype(jnp.bfloat16)
            return into

        def to_part(value):
            part[half] = value

        def to_own(value):
            own[half] = value

        quarter(half, (1 - yl) * 2 + 1 - c, to_near(0))
        near(half, 0).start()
        quarter(half, (1 - yl) * 2 + c, to_part)
        quarter(half, yl * 2 + 1 - c, to_near(1))
        near(half, 1).start()
        quarter(half, yl * 2 + c, to_own)

    def combine(half):
        near(half, 0).wait_recv()
        cross_out[half] = (part[half] + near_in[half, 0].astype(jnp.float32)).astype(jnp.bfloat16)
        cross(half).start()

    def begin_far(a, carry):
        begin_step(2 * a + 1, (8, 7, 6))
        return carry

    def begin_near(a, carry):
        begin_step(2 * a, (8, 2, 1, 0), ((2 * a + 1, 0),))
        return carry

    lax.fori_loop(0, 2, begin_far, 0)
    pass_below(shards[2])
    pass_below(shards[3])
    lax.fori_loop(2, 4, begin_far, 0)
    from_sibling(0)
    lax.fori_loop(0, 2, begin_near, 0)
    for shard in shards:
        pass_across(shard)
    lax.fori_loop(2, 4, begin_near, 0)
    from_sibling(1)
    w_copy.wait()
    fill(2, step_of(0), 3 - 2 * lax.rem(step_of(0), 2))

    def turn(n, carry):
        end_step(n)
        for e in range(2):
            is_self, copy, src, dst, recv = give_back(n, e)
            each_way(is_self, copy, src, dst, recv)

        @pl.when((lax.rem(n, 2) == 0) & (n > 0))
        def _():
            project(n // 2 - 1)

        @pl.when((lax.rem(n, 2) == 1) & (n > 1))
        def _():
            combine(n // 2 - 1)

        return carry

    lax.fori_loop(0, STEPS, turn, 0)
    project(3)
    combine(3)

    def out_copy(half):
        rows = pl.ds(half * PART, PART)
        return pltpu.make_async_copy(out_loc.at[rows], out_hbm.at[rows], out_sem.at[half])

    for half in range(4):
        near(half, 1).wait_recv()
        cross(half).wait_recv()
        out_loc[half * PART:(half + 1) * PART, :] = (
            own[half] + near_in[half, 1].astype(jnp.float32) + cross_in[half].astype(jnp.float32)
        ).astype(jnp.bfloat16)
        out_copy(half).start()

    for is_self, copy in exchanged:
        @pl.when(jnp.logical_not(is_self))
        def _():
            copy.wait_send()

    for shard in range(4):
        to_above(shard).wait_send()
        to_across(0, shard).wait_send()
        for slot in range(3):
            to_sibling(slot, shard).wait_send()
    for n in range(STEPS):
        for e in range(2):
            is_self, copy, _, _, _ = give_back(n, e)

            @pl.when(jnp.logical_not(is_self))
            def _():
                copy.wait_send()

    for half in range(4):
        out_copy(half).wait()
        near(half, 0).wait_send()
        near(half, 1).wait_send()
        cross(half).wait_send()


def on_device(queries, keys, values, lengths, out_weight):
    bf16, f32 = jnp.bfloat16, jnp.float32
    dma = pltpu.SemaphoreType.DMA
    anywhere = pl.BlockSpec(memory_space=pl.ANY)
    return pl.pallas_call(
        kernel,
        out_shape=jax.ShapeDtypeStruct((ROWS, 1024), bf16),
        in_specs=[pl.BlockSpec(memory_space=pltpu.SMEM)] + [anywhere] * 4,
        out_specs=anywhere,
        scratch_shapes=[
            pltpu.VMEM((ROWS, 1024), bf16),
            pltpu.VMEM((ROWS, 256), bf16),
            pltpu.VMEM((2, ROWS, HEAD), bf16),
            pltpu.VMEM((1024, 4096), bf16),
            pltpu.VMEM((2, WINDOW, HEAD), bf16),
            pltpu.VMEM((STEPS, HEAD, 512), bf16),
            pltpu.VMEM((STEPS, HEAD), jnp.int32),
            pltpu.VMEM((3, TILE, 512), f32),
            pltpu.VMEM((STEPS, HEAD + 16, 512), f32),
            pltpu.VMEM((STEPS, 1, 512), f32),
            pltpu.VMEM((STEPS, HEAD, 512), bf16),
            pltpu.VMEM((4, PART, 1024), bf16),
            pltpu.VMEM((4, 2, PART, 1024), bf16),
            pltpu.VMEM((4, 2, PART, 1024), bf16),
            pltpu.VMEM((4, PART, 1024), bf16),
            pltpu.VMEM((4, PART, 1024), bf16),
            pltpu.VMEM((4, PART, 1024), f32),
            pltpu.VMEM((4, PART, 1024), f32),
            dma((2,)),
            dma((2, 2)), dma((4,)),
            dma((4, 2, 2)), dma((STEPS, 2)),
            dma((4,)), dma((4,)),
            dma((4,)), dma((4,)),
            dma((3, 4)), dma((3, 4)),
            dma((STEPS, 2)), dma((4, 2, 2)),
            dma((4, 2)), dma((4, 2)),
            dma((4,)), dma((4,)), dma((4,)),
        ],
        compiler_params=pltpu.CompilerParams(
            collective_id=0, has_side_effects=True, vmem_limit_bytes=56 * 2**20
        ),
        name="attend_and_project",
    )(lengths, queries, keys, values, out_weight)


def solution(mesh):
    in_specs = (P("seq", "head"), P("seq", "head"), P("seq", "head"), P(), P("head", None))
    return jax.shard_map(
        on_device, mesh=mesh, in_specs=in_specs, out_specs=P("seq", "head"), check_vma=False
    )
```

time: 105 us -> 78.3 us (0.75)
  Pallas kernels: 103 us -> 75.9 us
    pallas_call x1, Pallas kernels: 103 us -> 75.9 us  [on_device(): pl.pallas_call(kernel, out_shape=jax.ShapeDtypeStruct((ROWS, 1024), bf16)...]
where the time goes in v2:
time: 78.3 us; the launch traced here: 78.2 us
  Pallas kernels  75.9 us (97%)
  local copies, waits for them, and re-layouts  2.26 us (3%)
    pallas_call x1, Pallas kernels, on_device(): pl.pallas_call(kernel, out_shape=jax.ShapeDtypeStruct((ROWS, 1024), bf16)...  75.9 us
    unnamed x1, local copies, waits for them, and re-layouts  2.26 us

profile of v2, /device:TPU:1, one launch (start us, length us, event | category | flops | bytes accessed | tf_op | source)
XLA Modules:
  0.0 78.2 jit_solution(14935262447232652305)
XLA Ops:
  0.0 75.9 %attend_and_project.1 = bf16[512,1024]{1,0:T(8,128)(2,1)} custom-call(s32[16]{0:T(128)} %len_ref.1, bf16[512,1024]{1,0:T(8,128)(2,1)} %q_hbm.1, bf16[512,256]{1,0:T(8,128)(2,1)} %k_hbm.1, bf16[512,256]{1,0:T(8,128)(2,1)} %v_hbm.1, bf16[1024,4096]{1,0:T(8,128)(2,1)} %w_hbm.1), custom_call_target="tpu_custom_call" | custom-call | tf_op jit(solution)/shard_map/attend_and_project/pallas_call | solution.py:401
  75.9 2.3 %copy.7 = bf16[512,1024]{1,0:T(8,128)(2,1)} copy(bf16[512,1024]{1,0:T(8,128)(2,1)} %attend_and_project.1) | data formatting | bytes 2097152

commit v3 on v2

--- a/solution.py
+++ b/solution.py
@@ -343,17 +343,18 @@
             is_self, copy, src, dst, recv = give_back(n, e)
             each_way(is_self, copy, src, dst, recv)
 
-        @pl.when((lax.rem(n, 2) == 0) & (n > 0))
+        @pl.when((n == 4) | (n == 6))
+        def _():
+            combine(n // 2 - 2)
+
+        @pl.when((n == 3) | (n == 5) | (n == 7))
         def _():
             project(n // 2 - 1)
 
-        @pl.when((lax.rem(n, 2) == 1) & (n > 1))
-        def _():
-            combine(n // 2 - 1)
-
         return carry
 
     lax.fori_loop(0, STEPS, turn, 0)
+    combine(2)
     project(3)
     combine(3)
 

time: 78.3 us -> 77.3 us (0.987)
  Pallas kernels: 75.9 us -> 74.9 us
    pallas_call x1, Pallas kernels: 75.9 us -> 74.9 us  [on_device(): pl.pallas_call(kernel, out_shape=jax.ShapeDtypeStruct((ROWS, 1024), bf16)...]
where the time goes in v3:
time: 77.3 us; the launch traced here: 77.2 us
  Pallas kernels  74.9 us (97%)
  local copies, waits for them, and re-layouts  2.26 us (3%)
    pallas_call x1, Pallas kernels, on_device(): pl.pallas_call(kernel, out_shape=jax.ShapeDtypeStruct((ROWS, 1024), bf16)...  74.9 us
    unnamed x1, local copies, waits for them, and re-layouts  2.26 us

profile of v3, /device:TPU:1, one launch (start us, length us, event | category | flops | bytes accessed | tf_op | source)
XLA Modules:
  0.0 77.2 jit_solution(10773333783233911291)
XLA Ops:
  0.0 74.9 %attend_and_project.1 = bf16[512,1024]{1,0:T(8,128)(2,1)} custom-call(s32[16]{0:T(128)} %len_ref.1, bf16[512,1024]{1,0:T(8,128)(2,1)} %q_hbm.1, bf16[512,256]{1,0:T(8,128)(2,1)} %k_hbm.1, bf16[512,256]{1,0:T(8,128)(2,1)} %v_hbm.1, bf16[1024,4096]{1,0:T(8,128)(2,1)} %w_hbm.1), custom_call_target="tpu_custom_call" | custom-call | tf_op jit(solution)/shard_map/attend_and_project/pallas_call | solution.py:402
  74.9 2.3 %copy.7 = bf16[512,1024]{1,0:T(8,128)(2,1)} copy(bf16[512,1024]{1,0:T(8,128)(2,1)} %attend_and_project.1) | data formatting | bytes 2097152
